TPU v7x, 32 devices: a whole 2x2x4 slice. The times are simulated.
32 devices in a mesh: exp: 4 (over y, core), seq: 2 (over x), dp: 4 (over z).
Axes of the slice: x: 2, y: 2, z: 4, core: 2. Of those that a mesh axis runs over, the one named last changes fastest.
Arguments:
- queries: bfloat16 [4, 256, 4, 2048], P('exp', None, 'dp', 'seq'), may hold values from -160 to 160
- latent_rows: bfloat16 [4, 256, 512], P('exp'), may hold values from -8 to 8
- key_weight: bfloat16 [512, 4, 2048], P(None, 'dp', 'seq'), may hold values from -1 to 1
- output_grad: bfloat16 [4, 256, 4, 2048], P('exp', 'seq', 'dp'), may hold values from -6 to 6
- down_weight: bfloat16 [4, 2048, 7168], P('exp', 'dp', 'seq'), may hold values from -0.125 to 0.125
- hidden_rows: bfloat16 [768, 2048], P('exp', 'dp'), may hold values from -6 to 6
- upstream_rows: bfloat16 [768, 7168], P('exp', 'seq'), may hold values from -6 to 6
- row_gates: float32 [768], P('exp'), may hold values from 0.03 to 0.5
- row_counts: int32 [4, 3], P('exp'), may hold values from 0 to 64, as said below
Outputs:
- value_grad: bfloat16 [4, 256, 4, 2048], P('exp', None, 'dp', 'seq')
- hidden_grad: float32 [768, 2048], P(('exp', 'seq'), 'dp')
- weight_grad: bfloat16 [4, 2048, 7168], P('exp', 'dp', 'seq')
Inputs may be any that keep to these rules, and one draw needn't show every extreme that they name: `row_counts`: A block with 0 live rows means host j keeps no copy of expert e(j, b); in every draw some block is full with 64 live rows.
All inputs are finite; a program needn't handle non-finite values.
Results may differ from a plain program's by a relative error of at most 0.012.
The roundings to bfloat16 on the way count: a program that leaves them out, or rounds other values in their place, can miss the bound.
Values may be sent and summed in bfloat16 or wider, within the bound.
A program may use at most 64 MiB of HBM per device.

v0:
```python
import math

import jax
import jax.numpy as jnp
from jax import lax
from jax.sharding import PartitionSpec as P

HEAD_DIM = 128


def shifted(block, axis, distance):
    devices = range(lax.axis_size(axis))
    route = [((i - distance) % len(devices), i) for i in devices]
    return lax.ppermute(block, axis, route)


def attend(queries, latent_rows, key_weight, head_grads):
    seq_len = queries.shape[1]
    feature_width = queries.shape[3]
    head_count = feature_width // HEAD_DIM
    key_rows = jnp.dot(
        latent_rows[0],
        key_weight.reshape(key_weight.shape[0], feature_width),
        preferred_element_type=jnp.float32,
    ).astype(jnp.bfloat16)
    key_heads = key_rows.reshape(seq_len, head_count, HEAD_DIM)
    query_heads = queries[0, :, 0, :].reshape(seq_len, head_count, HEAD_DIM)
    grad_heads = head_grads[0, :, 0, :].reshape(seq_len, head_count, HEAD_DIM)
    block_rows = max(min(512, seq_len), seq_len // 8)
    score_scale = 1.0 / math.sqrt(HEAD_DIM)
    accumulated = jnp.zeros((seq_len, head_count, HEAD_DIM), jnp.float32)
    for block_number in range(seq_len // block_rows):
        first_row = block_number * block_rows
        last_row = first_row + block_rows
        scores = (
            jnp.einsum(
                "qhd,khd->hqk",
                query_heads[first_row:last_row],
                key_heads[:last_row],
                preferred_element_type=jnp.float32,
            )
            * score_scale
        )
        allowed = jnp.arange(last_row)[None, :] <= (first_row + jnp.arange(block_rows))[:, None]
        scores = jnp.where(allowed[None], scores, -jnp.inf)
        row_max = jnp.max(scores, axis=2, keepdims=True)
        weights = jnp.exp(scores - row_max)
        softmax_rows = (weights / jnp.sum(weights, axis=2, keepdims=True)).astype(jnp.bfloat16)
        contribution = jnp.einsum(
            "hqk,qhd->khd",
            softmax_rows,
            grad_heads[first_row:last_row],
            preferred_element_type=jnp.float32,
        )
        accumulated = accumulated.at[:last_row].add(contribution)
    return accumulated.astype(jnp.bfloat16).reshape(1, seq_len, 1, feature_width)


def row_products(upstream, matrix):
    return jnp.einsum("rd,fd->rf", upstream, matrix, preferred_element_type=jnp.float32)


def term_product(scaled, upstream):
    return jnp.einsum("rf,rd->fd", scaled, upstream, preferred_element_type=jnp.float32).astype(
        jnp.bfloat16
    )


def expert_part(down_weight, hidden_rows, upstream_rows, row_gates, row_counts):
    own_tile = down_weight[0]
    capacity = hidden_rows.shape[0] // 3
    offset_step = lax.axis_size("exp") // 3
    live_rows = jnp.arange(capacity)[None, :] < row_counts[0][:, None]
    row_scale = jnp.where(live_rows, row_gates.reshape(3, capacity), 0.0).reshape(3 * capacity)
    scaled_rows = (row_scale[:, None] * hidden_rows.astype(jnp.float32)).astype(jnp.bfloat16)
    hidden_blocks = scaled_rows.reshape(3, capacity, scaled_rows.shape[1])
    upstream_blocks = upstream_rows.reshape(3, capacity, upstream_rows.shape[1])
    grad_blocks = [row_products(upstream_blocks[0], own_tile)]
    own_term = term_product(hidden_blocks[0], upstream_blocks[0])
    summed = lax.optimization_barrier(own_term).astype(jnp.float32)
    for block_index in (1, 2):
        moved_rows, moved_upstream = shifted(
            (hidden_blocks[block_index], upstream_blocks[block_index]),
            "exp",
            -block_index * offset_step,
        )
        block_term = term_product(moved_rows, moved_upstream)
        summed = summed + lax.optimization_barrier(block_term).astype(jnp.float32)
        partial_grad = row_products(moved_upstream, own_tile)
        grad_blocks.append(shifted(partial_grad, "exp", block_index * offset_step))
    grad_parts = jnp.concatenate(grad_blocks, 0) * row_scale[:, None]
    hidden_grad = lax.psum_scatter(grad_parts, "seq", scatter_dimension=0, tiled=True)
    weight_grad = summed.astype(jnp.bfloat16)[None]
    return (hidden_grad, weight_grad)


def on_device(
    queries,
    latent_rows,
    key_weight,
    output_grad,
    down_weight,
    hidden_rows,
    upstream_rows,
    row_gates,
    row_counts,
):
    head_grads = lax.all_to_all(output_grad, "seq", split_axis=3, concat_axis=1, tiled=True)
    hidden_grad, weight_grad = expert_part(
        down_weight, hidden_rows, upstream_rows, row_gates, row_counts
    )
    value_grad = attend(queries, latent_rows, key_weight, head_grads)
    return (value_grad, hidden_grad, weight_grad)


def solution(mesh):
    placed = (
        P("exp", None, "dp", "seq"),
        P("exp", None, None),
        P(None, "dp", "seq"),
        P("exp", "seq", "dp", None),
        P("exp", "dp", "seq"),
        P("exp", "dp"),
        P("exp", "seq"),
        P("exp"),
        P("exp", None),
    )
    return jax.shard_map(
        on_device,
        mesh=mesh,
        in_specs=placed,
        out_specs=(P("exp", None, "dp", "seq"), P(("exp", "seq"), "dp"), P("exp", "dp", "seq")),
        check_vma=False,
    )
```

profile of v0, /device:TPU:0, one launch (start us, length us, event | category | flops | bytes accessed | tf_op | source)
XLA Modules:
  0.0 85.3 jit_solution(17108053000998193302)
XLA Ops:
  7.2 0.0 copy-start
  7.2 0.0 copy-start.3
  7.2 2.3 %fusion.36 = (bf16[64,3584]{1,0:T(8,128)(2,1)}, bf16[64,3584]{1,0:T(8,128)(2,1)}) fusion(bf16[192,3584]{1,0:T(8,128)(2,1)} %param.19), kind=kLoop, calls=%fused_computation.38 | loop fusion | bytes 1835008 | tf_op jit(solution)/shard_map/slice | solution.py:83
  9.5 2.4 %collective-permute-start = (bf16[64,3584]{1,0:T(8,128)(2,1)}, bf16[64,3584]{1,0:T(8,128)(2,1)}, u32[]{:S(2)}, u32[]{:S(2)}) collective-permute-start(bf16[64,3584]{1,0:T(8,128)(2,1)} %get-tuple-element.32), channel_id=1, source_target_pairs={{8,0},{16,8},{24,16},{0,24},{9,1},{17,9},{25,17},{1,25},{10,2},{18... | collective-permute-start | bytes 1376264 | tf_op jit(solution)/shard_map/ppermute | solution.py:14
  11.9 0.6 collective-permute-start.2
  12.5 2.3 %copy.25 = bf16[1,128,1,2048]{1,2,0,3:T(2,128)(2,1)S(1)} copy(bf16[1,128,1,2048]{3,1,2,0:T(8,128)(2,1)} %param.16) | data formatting | bytes 1048576 | tf_op args[3]
  14.8 0.5 broadcast.51
  15.3 12.3 %reduce.2 = bf16[2048,128]{1,0:T(8,128)(2,1)} reduce(bf16[2048,1,1,128]{3,2,1,0:T(2,128)(2,1)S(1)} %bitcast.59, bf16[]{:T(256)} %broadcast.51), dimensions={1,2}, to_apply=%bitcast.45.reduce_sub_computation | reduce | bytes 1048578
  27.6 0.0 copy-start.4
  27.7 1.9 %reshape.99 = bf16[2,2,65536]{2,1,0:T(2,128)(2,1)} reshape(bf16[2048,128]{1,0:T(8,128)(2,1)} %reduce.2) | data formatting | bytes 1048576
  29.5 4.2 %all-to-all-start = ((bf16[2,2,65536]{2,1,0:T(2,128)(2,1)}), bf16[2,2,65536]{2,1,0:T(2,128)(2,1)}, u32[]{:S(2)}, u32[]{:S(2)}) async-start(bf16[2,2,65536]{2,1,0:T(2,128)(2,1)} %reshape.99), calls=%async_computation | async-start | bytes 1048576 | tf_op jit(solution)/shard_map/all_to_all | solution.py:108
  33.7 0.0 reduce-scatter.2.cloned.1.call-start
  33.8 0.0 copy-start.5
  33.8 0.0 copy-done.3
  33.9 4.0 %fusion.6 = f32[64,512]{1,0:T(8,128)} fusion(bf16[1,512,3584]{2,1,0:T(8,128)(2,1)} %param.17, bf16[192,3584]{1,0:T(8,128)(2,1)S(1)} %copy-done.3), kind=kOutput, calls=%fused_computation.10 | convolution fusion | flops 234881024 | bytes 4259840 | tf_op jit(solution)/shard_map/rd,fd->rf/dot_general | solution.py:60
  37.8 0.0 copy-done.4
  37.8 0.1 copy.32
  37.9 0.0 copy-done
  37.9 0.0 copy-done.5
  37.9 0.0 copy-start.7
  38.0 0.0 copy-start.6
  38.0 0.4 fusion.9
  38.4 2.1 %fusion.38 = (f32[8,256]{1,0:T(8,128)S(1)}, f32[8,256,256]{1,2,0:T(8,128)}) fusion(pred[256,256]{0,1:T(8,128)(4,1)S(1)} %iota_compare_fusion, bf16[256,8,128]{2,1,0:T(8,128)(2,1)S(1)} %bitcast.62, bf16[32,8,8,128]{3,2,1,0:T(8,128)(2,1)S(1)} %fusion.9), kind=kOutput, calls=%fused_computation.40 | convolution fusion | flops 136315136 | bytes 3219456 | tf_op jit(solution)/shard_map/sub | solution.py:47
  40.5 0.0 copy-done.7
  40.5 0.1 iota_compare_fusion.1
  40.6 0.1 lt.24
  40.7 0.0 copy-done.6
  40.7 1.8 %all-to-all-done = bf16[2,2,65536]{2,1,0:T(2,128)(2,1)} async-done(((bf16[2,2,65536]{2,1,0:T(2,128)(2,1)}), bf16[2,2,65536]{2,1,0:T(2,128)(2,1)}, u32[]{:S(2)}, u32[]{:S(2)}) %all-to-all-start) | async-done | bytes 524320 | tf_op jit(solution)/shard_map/all_to_all | solution.py:108
  42.5 1.4 %reshape.100 = bf16[2048,1,1,128]{3,2,1,0:T(2,128)(2,1)S(1)} reshape(bf16[2,2,65536]{2,1,0:T(2,128)(2,1)} %all-to-all-done) | data formatting | bytes 1048576
  43.9 0.1 copy.30
  44.0 0.5 copy.26
  44.5 0.3 reshape_squeeze.7
  44.9 0.0 copy-start.1
  44.9 0.0 copy-start.8
  44.9 0.0 collective-permute-done
  44.9 4.2 %fusion.4 = f32[64,512]{1,0:T(8,128)} fusion(bf16[64,3584]{1,0:T(8,128)(2,1)} %collective-permute-done, bf16[1,512,3584]{2,1,0:T(8,128)(2,1)} %param.17), kind=kOutput, calls=%fused_computation.8 | convolution fusion | flops 234881024 | bytes 4259840 | tf_op jit(solution)/shard_map/rd,fd->rf/dot_general | solution.py:60
  49.1 0.0 collective-permute-start.1
  49.1 0.0 collective-permute-done.2
  49.1 0.0 copy-done.1
  49.1 2.9 %fusion.2 = f32[64,512]{1,0:T(8,128)} fusion(bf16[64,3584]{1,0:T(8,128)(2,1)} %collective-permute-done.2, bf16[1,512,3584]{2,1,0:T(8,128)(2,1)S(1)} %copy-done.1), kind=kOutput, calls=%fused_computation.6 | convolution fusion | flops 234881024 | bytes 4259840 | tf_op jit(solution)/shard_map/rd,fd->rf/dot_general | solution.py:60
  52.0 0.3 collective-permute-start.3
  52.3 0.0 copy-done.8
  52.3 0.5 convolution_convert_fusion.4
  52.8 1.0 %copy.28 = bf16[1,256,1,1024]{3,1,2,0:T(8,128)(2,1)} copy(bf16[1,256,1,1024]{1,3,2,0:T(8,128)(2,1)S(1)} %bitcast.63) | data formatting | bytes 1048576
  53.8 0.0 collective-permute-done.1
  53.8 4.3 %collective-permute-done.3 = f32[64,512]{1,0:T(8,128)} collective-permute-done((f32[64,512]{1,0:T(8,128)}, f32[64,512]{1,0:T(8,128)}, u32[]{:S(2)}, u32[]{:S(2)}) %collective-permute-start.3) | collective-permute-done | bytes 131104 | tf_op jit(solution)/shard_map/ppermute | solution.py:14
  58.2 2.0 %multiply_convert_fusion = (bf16[192,512]{1,0:T(8,128)(2,1)S(1)}, f32[192,512]{1,0:T(8,128)}) fusion(bf16[192,512]{1,0:T(8,128)(2,1)} %param.18, f32[192]{0:T(256)S(1)} %broadcast_select_fusion, f32[64,512]{1,0:T(8,128)} %collective-permute-done.3, f32[64,512]{1,0:T(8,128)} %collective-permute-done.1, f32[64,512]{1,0:T(8,128)} %fusion.6), kind=kLoop, calls=%fused_computation.30 | loop fusion | flops 589824 | bytes 1180416 | tf_op jit(solution)/shard_map/convert_element_type | solution.py:75
  60.2 0.5 collective-permute-start.4
  60.6 3.0 %convolution_convert_fusion.2 = bf16[512,3584]{1,0:T(8,128)(2,1)} fusion(bf16[192,3584]{1,0:T(8,128)(2,1)S(1)} %copy-done.3, bf16[192,512]{1,0:T(8,128)(2,1)S(1)} %get-tuple-element.36), kind=kOutput, calls=%fused_computation.4 | convolution fusion | flops 236716032 | bytes 4194304 | tf_op jit(solution)/shard_map/rf,rd->fd/dot_general | solution.py:64
  63.6 1.0 %collective-permute-start.5 = (bf16[64,512]{1,0:T(8,128)(2,1)S(1)}, bf16[64,512]{1,0:T(8,128)(2,1)S(1)}, u32[]{:S(2)}, u32[]{:S(2)}) collective-permute-start(bf16[64,512]{1,0:T(8,128)(2,1)S(1)} %get-tuple-element.35), channel_id=1, source_target_pairs={{16,0},{24,8},{0,16},{8,24},{17,1},{25,9},{1,17},{9,25},{18,2},{26... | collective-permute-start | bytes 196616 | tf_op jit(solution)/shard_map/ppermute | solution.py:14
  64.6 0.0 reduce-scatter.2.cloned.1.call-update
  64.7 0.0 copy-start.2
  64.7 0.0 collective-permute-done.4
  64.7 2.3 %convolution_convert_fusion.1 = bf16[512,3584]{1,0:T(8,128)(2,1)S(1)} fusion(bf16[64,512]{1,0:T(8,128)(2,1)S(1)} %collective-permute-done.4, bf16[64,3584]{1,0:T(8,128)(2,1)} %collective-permute-done), kind=kOutput, calls=%fused_computation.3 | convolution fusion | flops 236716032 | bytes 4194304 | tf_op jit(solution)/shard_map/rf,rd->fd/dot_general | solution.py:64
  67.0 0.9 %collective-permute-done.5 = bf16[64,512]{1,0:T(8,128)(2,1)S(1)} collective-permute-done((bf16[64,512]{1,0:T(8,128)(2,1)S(1)}, bf16[64,512]{1,0:T(8,128)(2,1)S(1)}, u32[]{:S(2)}, u32[]{:S(2)}) %collective-permute-start.5) | collective-permute-done | bytes 65568 | tf_op jit(solution)/shard_map/ppermute | solution.py:14
  67.9 2.2 %convolution_convert_fusion = bf16[512,3584]{1,0:T(8,128)(2,1)S(1)} fusion(bf16[64,512]{1,0:T(8,128)(2,1)S(1)} %collective-permute-done.5, bf16[64,3584]{1,0:T(8,128)(2,1)} %collective-permute-done.2), kind=kOutput, calls=%fused_computation.2 | convolution fusion | flops 236716032 | bytes 4194304 | tf_op jit(solution)/shard_map/rf,rd->fd/dot_general | solution.py:64
  70.0 0.0 copy-done.2
  70.0 3.2 %fusion.1 = bf16[1,512,3584]{2,1,0:T(8,128)(2,1)} fusion(bf16[512,3584]{1,0:T(8,128)(2,1)S(1)} %convolution_convert_fusion, bf16[512,3584]{1,0:T(8,128)(2,1)S(1)} %convolution_convert_fusion.1, bf16[512,3584]{1,0:T(8,128)(2,1)S(1)} %copy-done.2), kind=kLoop, calls=%fused_computation.5 | loop fusion | flops 11010048 | bytes 14680064 | tf_op jit(solution)/shard_map/broadcast_in_dim | solution.py:93
  73.2 5.2 %reduce-scatter.2.cloned.1.call-done = f32[96,512]{1,0:T(8,128)} async-done(((f32[192,512]{1,0:T(8,128)}), f32[96,512]{1,0:T(8,128)}) %reduce-scatter.2.cloned.1.call-update) | async-done | bytes 196624 | tf_op jit(solution)/shard_map/reduce_scatter | solution.py:92
  (3 shorter events, 0.0 us)
Async XLA Ops:
  7.2 30.8 %copy-start = (bf16[512,1,1024]{2,0,1:T(8,128)(2,1)S(1)}, bf16[512,1,1024]{2,0,1:T(8,128)(2,1)}, u32[]{:S(2)}) copy-start(bf16[512,1,1024]{2,0,1:T(8,128)(2,1)} %param.15) | copy-start | bytes 3145732
  7.2 26.7 %copy-start.3 = (bf16[192,3584]{1,0:T(8,128)(2,1)S(1)}, bf16[192,3584]{1,0:T(8,128)(2,1)}, u32[]{:S(2)}) copy-start(bf16[192,3584]{1,0:T(8,128)(2,1)} %param.19) | copy-start | bytes 4128772
  9.5 35.4 %collective-permute-start = (bf16[64,3584]{1,0:T(8,128)(2,1)}, bf16[64,3584]{1,0:T(8,128)(2,1)}, u32[]{:S(2)}, u32[]{:S(2)}) collective-permute-start(bf16[64,3584]{1,0:T(8,128)(2,1)} %get-tuple-element.32), channel_id=1, source_target_pairs={{8,0},{16,8},{24,16},{0,24},{9,1},{17,9},{25,17},{1,25},{10,2},{18... | collective-permute-start | bytes 1376264 | tf_op jit(solution)/shard_map/ppermute | solution.py:14
  11.9 37.2 %collective-permute-start.2 = (bf16[64,3584]{1,0:T(8,128)(2,1)}, bf16[64,3584]{1,0:T(8,128)(2,1)}, u32[]{:S(2)}, u32[]{:S(2)}) collective-permute-start(bf16[64,3584]{1,0:T(8,128)(2,1)} %get-tuple-element.33), channel_id=1, source_target_pairs={{16,0},{24,8},{0,16},{8,24},{17,1},{25,9},{1,17},{9,25},{18,2},{26... | collective-permute-start | bytes 1376264 | tf_op jit(solution)/shard_map/ppermute | solution.py:14
  27.6 10.2 %copy-start.4 = (bf16[1,256,1,1024]{3,1,2,0:T(8,128)(2,1)S(1)}, bf16[1,256,1,1024]{3,1,2,0:T(8,128)(2,1)}, u32[]{:S(2)}) copy-start(bf16[1,256,1,1024]{3,1,2,0:T(8,128)(2,1)} %param.13) | copy-start | bytes 1572868
  29.5 13.0 %all-to-all-start = ((bf16[2,2,65536]{2,1,0:T(2,128)(2,1)}), bf16[2,2,65536]{2,1,0:T(2,128)(2,1)}, u32[]{:S(2)}, u32[]{:S(2)}) async-start(bf16[2,2,65536]{2,1,0:T(2,128)(2,1)} %reshape.99), calls=%async_computation | async-start | bytes 1048576 | tf_op jit(solution)/shard_map/all_to_all | solution.py:108
  33.7 44.7 %reduce-scatter.2.cloned.1.call-start = ((), (), s32[]{:S(2)}) async-start(), calls=%async_computation.2 | async-start | bytes 589824 | tf_op jit(solution)/shard_map/reduce_scatter | solution.py:92
  33.8 4.1 %copy-start.5 = (bf16[1,256,512]{2,1,0:T(8,128)(2,1)S(1)}, bf16[1,256,512]{2,1,0:T(8,128)(2,1)}, u32[]{:S(2)}) copy-start(bf16[1,256,512]{2,1,0:T(8,128)(2,1)} %param.14) | copy-start | bytes 786436
  37.9 2.6 %copy-start.7 = (s32[1,3]{1,0:T(1,128)S(1)}, s32[1,3]{1,0:T(1,128)}, u32[]{:S(2)}) copy-start(s32[1,3]{1,0:T(1,128)} %param.21) | copy-start | bytes 40
  38.0 2.8 %copy-start.6 = (f32[192]{0:T(256)S(1)}, f32[192]{0:T(256)}, u32[]{:S(2)}) copy-start(f32[192]{0:T(256)} %param.20) | copy-start | bytes 2308
  44.9 4.2 %copy-start.1 = (bf16[1,512,3584]{2,1,0:T(8,128)(2,1)S(1)}, bf16[1,512,3584]{2,1,0:T(8,128)(2,1)}, u32[]{:S(2)}) copy-start(bf16[1,512,3584]{2,1,0:T(8,128)(2,1)} %param.17) | copy-start | bytes 11010052
  44.9 7.4 %copy-start.8 = (f32[8,256,256]{1,2,0:T(8,128)S(1)}, f32[8,256,256]{1,2,0:T(8,128)}, u32[]{:S(2)}) copy-start(f32[8,256,256]{1,2,0:T(8,128)} %get-tuple-element.39) | copy-start | bytes 6291460
  49.1 4.7 %collective-permute-start.1 = (f32[64,512]{1,0:T(8,128)}, f32[64,512]{1,0:T(8,128)}, u32[]{:S(2)}, u32[]{:S(2)}) collective-permute-start(f32[64,512]{1,0:T(8,128)} %fusion.4), channel_id=1, source_target_pairs={{24,0},{0,8},{8,16},{16,24},{25,1},{1,9},{9,17},{17,25},{26,2},{2,... | collective-permute-start | bytes 393224 | tf_op jit(solution)/shard_map/ppermute | solution.py:14
  52.0 6.1 %collective-permute-start.3 = (f32[64,512]{1,0:T(8,128)}, f32[64,512]{1,0:T(8,128)}, u32[]{:S(2)}, u32[]{:S(2)}) collective-permute-start(f32[64,512]{1,0:T(8,128)} %fusion.2), channel_id=1, source_target_pairs={{16,0},{24,8},{0,16},{8,24},{17,1},{25,9},{1,17},{9,25},{18,2},{26... | collective-permute-start | bytes 393224 | tf_op jit(solution)/shard_map/ppermute | solution.py:14
  60.2 4.5 %collective-permute-start.4 = (bf16[64,512]{1,0:T(8,128)(2,1)S(1)}, bf16[64,512]{1,0:T(8,128)(2,1)S(1)}, u32[]{:S(2)}, u32[]{:S(2)}) collective-permute-start(bf16[64,512]{1,0:T(8,128)(2,1)S(1)} %get-tuple-element.34), channel_id=1, source_target_pairs={{8,0},{16,8},{24,16},{0,24},{9,1},{17,9},{25,17},{1,25},{10,2},{18... | collective-permute-start | bytes 196616 | tf_op jit(solution)/shard_map/ppermute | solution.py:14
  63.6 4.3 %collective-permute-start.5 = (bf16[64,512]{1,0:T(8,128)(2,1)S(1)}, bf16[64,512]{1,0:T(8,128)(2,1)S(1)}, u32[]{:S(2)}, u32[]{:S(2)}) collective-permute-start(bf16[64,512]{1,0:T(8,128)(2,1)S(1)} %get-tuple-element.35), channel_id=1, source_target_pairs={{16,0},{24,8},{0,16},{8,24},{17,1},{25,9},{1,17},{9,25},{18,2},{26... | collective-permute-start | bytes 196616 | tf_op jit(solution)/shard_map/ppermute | solution.py:14
  64.7 5.4 %copy-start.2 = (bf16[512,3584]{1,0:T(8,128)(2,1)S(1)}, bf16[512,3584]{1,0:T(8,128)(2,1)}, u32[]{:S(2)}) copy-start(bf16[512,3584]{1,0:T(8,128)(2,1)} %convolution_convert_fusion.2) | copy-start | bytes 11010052
Sparse Core Ops, SparseCore 0:
  64.8 13.6 reduce-scatter.1
where the time goes:
time: 85.7 us; the launch traced here: 85.3 us
  matrix products  21.5 us (25%)
  other arithmetic  17.6 us (21%)
  between operations  14.3 us (17%)
  waiting for transfers between devices  12.3 us (14%)
  local copies, waits for them, and re-layouts  10.7 us (12%)
  starting transfers between devices  9 us (11%)
    unnamed x1, other arithmetic  12.3 us
    dot_general x3, matrix products, row_products(): jnp.einsum('rd,fd->rf', upstream, matrix, preferred_element_type=jnp.floa...  11 us
    dot_general x3, matrix products, term_product(): jnp.einsum('rf,rd->fd', scaled, upstream, preferred_element_type=jnp.floa...  7.43 us
    unnamed x25, local copies, waits for them, and re-layouts  7.39 us
    ppermute x6, waiting for transfers between devices, shifted(): return lax.ppermute(block, axis, route)  5.25 us
    reduce_scatter x1, waiting for transfers between devices, expert_part(): lax.psum_scatter(grad_parts, 'seq', scatter_dimension=0, tiled=True)  5.22 us
    ppermute x6, starting transfers between devices, shifted(): return lax.ppermute(block, axis, route)  4.75 us
    all_to_all x1, starting transfers between devices, on_device(): lax.all_to_all(output_grad, 'seq', split_axis=3, concat_axis=1, tiled=True)  4.21 us
  transfers between devices with their start and end apart: 8, of which 4 were waited for; matrix products, arithmetic and copies ran while one was open for 53% of the time, Pallas kernels for 0%

commit v1 on v0

v1 whole, which is shorter than its diff:
```python
import functools
import math

import jax
import jax.numpy as jnp
from jax import lax
from jax.experimental import pallas as pl
from jax.experimental.pallas import tpu as pltpu
from jax.sharding import PartitionSpec as P

HEAD_DIM = 128
BLOCKS = 3
MESH = pl.DeviceIdType.MESH
LAST = (((1,), (1,)), ((), ()))


def dot_of(a, b):
    return jnp.dot(a, b, preferred_element_type=jnp.float32)


def grad_groups(capacity, rows_per):
    granule = math.gcd(capacity, rows_per)
    groups = []
    for block in range(BLOCKS):
        row, end = block * capacity, (block + 1) * capacity
        while row < end:
            owner = row // rows_per
            stop = min(end, (owner + 1) * rows_per)
            groups.append(
                (block, row // granule, (stop - row) // granule, owner,
                 (row - owner * rows_per) // granule)
            )
            row = stop
    return granule, groups


def kernel(
    n_exp, n_seq, chunks, tile, granule, groups,
    q_ref, lat_ref, kw_ref, og_ref, w_ref, hid_ref, up_ref, gate_ref, cnt_ref,
    vg_ref, hg_ref, wg_ref,
    q_v, lat_v, kw_v, g_v, w_v, hid_v, ups, own_sc, sc, sc_t, scale_v, acc, part, recv,
    load_sem, og_send, og_recv, up_send, up_recv, sc_send, sc_recv, part_send, part_recv,
):
    exp, seq = lax.axis_index("exp"), lax.axis_index("seq")
    step = n_exp // BLOCKS
    rows = hid_ref.shape[0]
    cap = rows // BLOCKS
    rows_per = rows // n_seq
    tokens, width = og_ref.shape[0], q_ref.shape[1]
    seq_len = q_ref.shape[0]

    def expert_at(distance):
        return lax.rem(exp + (distance % n_exp), n_exp)

    def seq_at(distance):
        return lax.rem(seq + (distance % n_seq), n_seq)

    offsets = sorted({(b * step * sign) % n_exp for b in range(BLOCKS) for sign in (1, -1)})
    partners = [(e, s) for e in offsets for s in range(n_seq) if (e, s) != (0, 0)]
    barrier = pltpu.get_barrier_semaphore()
    for e, s in partners:
        pl.semaphore_signal(
            barrier, inc=1, device_id={"exp": expert_at(e), "seq": seq_at(s)}, device_id_type=MESH
        )

    own_columns = pl.ds(pl.multiple_of(seq * width, width), width)
    own_tokens = pl.ds(pl.multiple_of(seq * tokens, tokens), tokens)
    loads = [
        pltpu.make_async_copy(hid_ref, hid_v, load_sem.at[0]),
        pltpu.make_async_copy(lat_ref, lat_v, load_sem.at[1]),
        pltpu.make_async_copy(kw_ref, kw_v, load_sem.at[2]),
        pltpu.make_async_copy(q_ref, q_v, load_sem.at[3]),
        pltpu.make_async_copy(og_ref.at[:, own_columns], g_v.at[own_tokens, :], load_sem.at[4]),
        pltpu.make_async_copy(up_ref.at[pl.ds(0, cap), :], ups.at[pl.ds(0, cap), :], load_sem.at[5]),
        pltpu.make_async_copy(w_ref, w_v, load_sem.at[6]),
    ]
    for load in loads:
        load.start()
    pl.semaphore_wait(barrier, len(partners))

    up_copies = []
    for c, (start, size) in enumerate(chunks):
        pair = []
        for b in (1, 2):
            place = (pl.ds(b * cap, cap), pl.ds(start, size))
            copy = pltpu.make_async_remote_copy(
                src_ref=up_ref.at[place], dst_ref=ups.at[place],
                send_sem=up_send.at[c, b - 1], recv_sem=up_recv.at[c, b - 1],
                device_id={"exp": expert_at(-b * step)}, device_id_type=MESH,
            )
            copy.start()
            pair.append(copy)
        up_copies.append(pair)
    og_copies = []
    for k in range(1, n_seq):
        other = seq_at(k)
        copy = pltpu.make_async_remote_copy(
            src_ref=og_ref.at[:, pl.ds(pl.multiple_of(other * width, width), width)],
            dst_ref=g_v.at[own_tokens, :],
            send_sem=og_send.at[k - 1], recv_sem=og_recv.at[k - 1],
            device_id={"seq": other}, device_id_type=MESH,
        )
        copy.start()
        og_copies.append(copy)

    loads[0].wait()
    line = lax.broadcasted_iota(jnp.int32, (rows, rows), 0)
    column = lax.broadcasted_iota(jnp.int32, (rows, rows), 1)
    gates = jnp.where(line == column, gate_ref[...], 0.0).sum(axis=1, keepdims=True)
    row = lax.broadcasted_iota(jnp.int32, (rows, 1), 0)
    limit = jnp.zeros((rows, 1), jnp.int32) + cnt_ref[0, 0]
    for b in range(1, BLOCKS):
        limit = jnp.where(row >= b * cap, b * cap + cnt_ref[0, b], limit)
    scale = jnp.where(row < limit, gates, 0.0)
    scale_v[...] = jnp.broadcast_to(scale, scale_v.shape)
    own_sc[...] = (scale * hid_v[...].astype(jnp.float32)).astype(jnp.bfloat16)
    sc_copies = []
    for b in (1, 2):
        place = pl.ds(b * cap, cap)
        copy = pltpu.make_async_remote_copy(
            src_ref=own_sc.at[place, :], dst_ref=sc.at[place, :],
            send_sem=sc_send.at[b - 1], recv_sem=sc_recv.at[b - 1],
            device_id={"exp": expert_at(-b * step)}, device_id_type=MESH,
        )
        copy.start()
        sc_copies.append(copy)
    sc[pl.ds(0, cap), :] = own_sc[pl.ds(0, cap), :]

    for load in loads[1:5]:
        load.wait()
    for copy in og_copies:
        copy.wait_recv()
    t_rows = min(256, seq_len)
    factor = 1.0 / math.sqrt(HEAD_DIM)

    @pl.loop(0, width // 256)
    def _(pair):
        columns = pl.ds(pl.multiple_of(pair * 256, 256), 256)
        keys = dot_of(lat_v[...], kw_v[:, columns]).astype(jnp.bfloat16)
        for half in range(2):
            head = pl.ds(pl.multiple_of(pair * 256 + half * HEAD_DIM, HEAD_DIM), HEAD_DIM)
            k_head = keys[:, half * HEAD_DIM : (half + 1) * HEAD_DIM]
            for first in range(0, seq_len, t_rows):
                last = first + t_rows
                q_head = q_v[pl.ds(first, t_rows), head]
                scores = lax.dot_general(
                    k_head[:last], q_head, LAST, preferred_element_type=jnp.float32
                ) * factor
                u = lax.broadcasted_iota(jnp.int32, scores.shape, 0)
                t = lax.broadcasted_iota(jnp.int32, scores.shape, 1) + first
                scores = jnp.where(u <= t, scores, -jnp.inf)
                weights = jnp.exp(scores - scores.max(axis=0, keepdims=True))
                probs = weights * (1.0 / weights.sum(axis=0, keepdims=True))
                term = dot_of(probs.astype(jnp.bfloat16), g_v[pl.ds(first, t_rows), head])
                total = term if first == 0 else term + jnp.concatenate(
                    [total, jnp.zeros((t_rows, HEAD_DIM), jnp.float32)], 0
                )
            vg_ref[:, head] = total.astype(jnp.bfloat16)

    loads[5].wait()
    loads[6].wait()
    for c, (start, size) in enumerate(chunks):
        for copy in up_copies[c]:
            copy.wait_recv()
        columns = pl.ds(start, size)
        product = lax.dot_general(
            ups[:, columns], w_v[:, columns], LAST, preferred_element_type=jnp.float32
        )
        acc[...] = product if c == 0 else acc[...] + product
    part[...] = acc[...].reshape(part.shape).astype(jnp.bfloat16)

    def group_copy(n):
        block, first, count, owner, place = groups[n]
        return pltpu.make_async_remote_copy(
            src_ref=part.at[pl.ds(first, count)],
            dst_ref=recv.at[seq, pl.ds(place, count)],
            send_sem=part_send.at[n], recv_sem=part_recv.at[seq, n],
            device_id={"exp": expert_at(block * step), "seq": owner}, device_id_type=MESH,
        )

    def arrival(n, source):
        block, first, count, owner, place = groups[n]
        return pltpu.make_async_remote_copy(
            src_ref=part.at[pl.ds(first, count)],
            dst_ref=recv.at[source, pl.ds(place, count)],
            send_sem=part_send.at[n], recv_sem=part_recv.at[source, n],
            device_id={"exp": expert_at(block * step), "seq": owner}, device_id_type=MESH,
        )

    for n in reversed(range(len(groups))):
        block, first, count, owner, place = groups[n]
        if block:
            group_copy(n).start()
        else:
            @pl.when(seq != owner)
            def _():
                group_copy(n).start()

            @pl.when(seq == owner)
            def _():
                recv[seq, pl.ds(place, count)] = part[pl.ds(first, count)]

    for copy in sc_copies:
        copy.wait_recv()
    sc_t[...] = sc[...].astype(jnp.float32).T.astype(jnp.bfloat16)

    @pl.loop(0, w_ref.shape[1] // tile)
    def _(n):
        columns = pl.ds(pl.multiple_of(n * tile, tile), tile)
        wg_ref[:, columns] = dot_of(sc_t[...], ups[:, columns]).astype(jnp.bfloat16)

    for n, (block, first, count, owner, place) in enumerate(groups):
        for source in range(n_seq):
            wanted = (seq == owner) if block else (seq == owner) & (seq != source)

            @pl.when(wanted)
            def _():
                arrival(n, source).wait_recv()
    total = recv[0].astype(jnp.float32)
    for source in range(1, n_seq):
        total = total + recv[source].astype(jnp.float32)
    own_rows = pl.ds(pl.multiple_of(seq * rows_per, 8), rows_per)
    hg_ref[...] = total.reshape(hg_ref.shape) * scale_v[own_rows, :][:, :1]

    for n, (block, first, count, owner, place) in enumerate(groups):
        if block:
            group_copy(n).wait_send()
        else:
            @pl.when(seq != owner)
            def _():
                group_copy(n).wait_send()
    for copy in sc_copies + og_copies + [c for pair in up_copies for c in pair]:
        copy.wait_send()


def on_device(
    queries, latent_rows, key_weight, output_grad, down_weight, hidden_rows, upstream_rows,
    row_gates, row_counts,
):
    n_exp, n_seq = lax.axis_size("exp"), lax.axis_size("seq")
    seq_len, width = queries.shape[1], queries.shape[3]
    tokens, latent = output_grad.shape[1], latent_rows.shape[2]
    hidden, model = down_weight.shape[1:]
    rows = hidden_rows.shape[0]
    rows_per = rows // n_seq
    granule, groups = grad_groups(rows // BLOCKS, rows_per)
    size = 512 if model % 512 == 0 else model
    tile = 512 if model % 512 == 0 else 128
    chunks = [(start, size) for start in range(0, model, size)]
    bf16, f32 = jnp.bfloat16, jnp.float32
    anywhere = pl.BlockSpec(memory_space=pltpu.HBM)
    vmem = pl.BlockSpec(memory_space=pltpu.VMEM)
    smem = pl.BlockSpec(memory_space=pltpu.SMEM)
    dma = pltpu.SemaphoreType.DMA
    value_grad, hidden_grad, weight_grad = pl.pallas_call(
        functools.partial(kernel, n_exp, n_seq, chunks, tile, granule, groups),
        out_shape=(
            pltpu.VMEM((seq_len, width), bf16),
            pltpu.VMEM((rows_per, hidden), f32),
            pltpu.VMEM((hidden, model), bf16),
        ),
        in_specs=[anywhere] * 7 + [vmem, smem],
        out_specs=(vmem,) * 3,
        scratch_shapes=[
            pltpu.VMEM((seq_len, width), bf16),
            pltpu.VMEM((seq_len, latent), bf16),
            pltpu.VMEM((latent, width), bf16),
            pltpu.VMEM((seq_len, width), bf16),
            pltpu.VMEM((hidden, model), bf16),
            pltpu.VMEM((rows, hidden), bf16),
            pltpu.VMEM((rows, model), bf16),
            pltpu.VMEM((rows, hidden), bf16),
            pltpu.VMEM((rows, hidden), bf16),
            pltpu.VMEM((hidden, rows), bf16),
            pltpu.VMEM((rows, 128), f32),
            pltpu.VMEM((rows, hidden), f32),
            pltpu.VMEM((rows // granule, granule, hidden), bf16),
            pltpu.VMEM((n_seq, rows_per // granule, granule, hidden), bf16),
            dma((7,)),
            dma((n_seq - 1,)),
            dma((n_seq - 1,)),
            dma((len(chunks), 2)),
            dma((len(chunks), 2)),
            dma((2,)),
            dma((2,)),
            dma((len(groups),)),
            dma((n_seq, len(groups))),
        ],
        compiler_params=pltpu.CompilerParams(
            collective_id=0, has_side_effects=True, vmem_limit_bytes=59 * 1024 * 1024
        ),
    )(
        queries.reshape(seq_len, width), latent_rows[0], key_weight.reshape(latent, width),
        output_grad.reshape(tokens, output_grad.shape[3]), down_weight[0], hidden_rows,
        upstream_rows, row_gates.reshape(1, rows), row_counts,
    )
    return (
        value_grad.reshape(1, seq_len, 1, width),
        hidden_grad,
        weight_grad[None],
    )


def solution(mesh):
    placed = (
        P("exp", None, "dp", "seq"),
        P("exp", None, None),
        P(None, "dp", "seq"),
        P("exp", "seq", "dp", None),
        P("exp", "dp", "seq"),
        P("exp", "dp"),
        P("exp", "seq"),
        P("exp"),
        P("exp", None),
    )
    return jax.shard_map(
        on_device,
        mesh=mesh,
        in_specs=placed,
        out_specs=(P("exp", None, "dp", "seq"), P(("exp", "seq"), "dp"), P("exp", "dp", "seq")),
        check_vma=False,
    )
```

time: 85.7 us -> 30.2 us (0.35)
  Pallas kernels: 0 us -> 26.1 us
  matrix products: 21.5 us -> 0 us
  other arithmetic: 17.6 us -> 0 us
  between operations: 14.3 us -> 0.64 us
  waiting for transfers between devices: 12.3 us -> 0 us
  starting transfers between devices: 9 us -> 0 us
  local copies, waits for them, and re-layouts: 10.7 us -> 3.31 us
    pallas_call x0 -> x1, Pallas kernels: none -> 26.1 us  [on_device(): pl.pallas_call(functools.partial(kernel, n_exp, n_seq, chunks, tile, gran...]
    dot_general x8 -> x0, matrix products: 19.4 us -> none  [the longest x3 11 us: row_products(): jnp.einsum('rd,fd->rf', upstream, matrix, preferred_element_type=jnp.floa...]
    unnamed x1 -> x0, other arithmetic: 12.3 us -> none
    ppermute x6 -> x0, waiting for transfers between devices: 5.25 us -> none  [shifted(): return lax.ppermute(block, axis, route)]
    reduce_scatter x1 -> x0, waiting for transfers between devices: 5.22 us -> none  [expert_part(): lax.psum_scatter(grad_parts, 'seq', scatter_dimension=0, tiled=True)]
    ppermute x6 -> x0, starting transfers between devices: 4.75 us -> none  [shifted(): return lax.ppermute(block, axis, route)]
    all_to_all x1 -> x0, starting transfers between devices: 4.21 us -> none  [on_device(): lax.all_to_all(output_grad, 'seq', split_axis=3, concat_axis=1, tiled=True)]
    unnamed x25 -> x3, local copies, waits for them, and re-layouts: 7.39 us -> 3.31 us
  transfers between devices with their start and end apart: 8 -> 0, of which waited for: 4 -> 0; matrix products, arithmetic and copies ran while one was open for 53% -> 0% of each run, Pallas kernels for 0% -> 0%
where the time goes in v1:
time: 30.2 us; the launch traced here: 30.1 us
  Pallas kernels  26.1 us (86%)
  local copies, waits for them, and re-layouts  3.31 us (11%)
  between operations  0.64 us (2%)
    pallas_call x1, Pallas kernels, on_device(): pl.pallas_call(functools.partial(kernel, n_exp, n_seq, chunks, tile, gran...  26.1 us
    unnamed x3, local copies, waits for them, and re-layouts  3.31 us

profile of v1, /device:TPU:0, one launch (start us, length us, event | category | flops | bytes accessed | tf_op | source)
XLA Modules:
  0.0 30.1 jit_solution(4177114187555908101)
XLA Ops:
  0.6 26.1 %shard_map.112 = (bf16[256,1024]{1,0:T(8,128)(2,1)S(1)}, f32[96,512]{1,0:T(8,128)S(1)}, bf16[512,3584]{1,0:T(8,128)(2,1)S(1)}) custom-call(bf16[256,1024]{1,0:T(8,128)(2,1)} %bitcast.12, bf16[256,512]{1,0:T(8,128)(2,1)} %bitcast.14, bf16[512,1024]{1,0:T(8,128)(2,1)} %bitcast.11, bf16[128,2048]{1,0:T(8,128)(2,1)} %bitcast.13, bf16[512,3584]{1,0:T(8,128)(2,1)} %bitcast.10, ...), custom_call_target="tpu_custom_call" | custom-call | tf_op jit(solution)/shard_map/pallas_call | solution.py:255
  26.7 0.8 %copy.15 = bf16[1,256,1,1024]{3,1,2,0:T(8,128)(2,1)} copy(bf16[1,256,1,1024]{3,1,2,0:T(8,128)(2,1)S(1)} %bitcast.9) | data formatting | bytes 1048576
  27.5 0.7 %copy.16 = f32[96,512]{1,0:T(8,128)} copy(f32[96,512]{1,0:T(8,128)S(1)} %get-tuple-element.10) | data formatting | bytes 393216
  28.2 1.8 %copy.17 = bf16[1,512,3584]{2,1,0:T(8,128)(2,1)} copy(bf16[1,512,3584]{2,1,0:T(8,128)(2,1)S(1)} %bitcast.8) | data formatting | bytes 7340032

commit v2 on v1

--- a/solution.py
+++ b/solution.py
@@ -35,13 +35,13 @@
 
 
 def kernel(
-    n_exp, n_seq, chunks, tile, granule, groups,
+    n_exp, n_seq, size, tile, granule, groups,
     q_ref, lat_ref, kw_ref, og_ref, w_ref, hid_ref, up_ref, gate_ref, cnt_ref,
     vg_ref, hg_ref, wg_ref,
-    q_v, lat_v, kw_v, g_v, w_v, hid_v, ups, own_sc, sc, sc_t, scale_v, acc, part, recv,
-    load_sem, og_send, og_recv, up_send, up_recv, sc_send, sc_recv, part_send, part_recv,
+    q_v, lat_v, kw_v, g_v, w_v, hid_v, ups, own_sc, sc, sc_t, scale_v, acc, part, recv, probs_v,
+    load_sem, og_send, og_recv, up_send, up_recv, near_send, far_send, far_recv, sc_send, sc_recv, part_send, part_recv,
 ):
-    exp, seq = lax.axis_index("exp"), lax.axis_index("seq")
+    exp, seq, dp = lax.axis_index("exp"), lax.axis_index("seq"), lax.axis_index("dp")
     step = n_exp // BLOCKS
     rows = hid_ref.shape[0]
     cap = rows // BLOCKS
@@ -57,7 +57,11 @@
 
     offsets = sorted({(b * step * sign) % n_exp for b in range(BLOCKS) for sign in (1, -1)})
     partners = [(e, s) for e in offsets for s in range(n_seq) if (e, s) != (0, 0)]
+    side = lax.rem(dp, 2)
+    mate = dp + 1 - 2 * side
+    n_chunks = w_ref.shape[1] // size
     barrier = pltpu.get_barrier_semaphore()
+    pl.semaphore_signal(barrier, inc=1, device_id={"dp": mate}, device_id_type=MESH)
     for e, s in partners:
         pl.semaphore_signal(
             barrier, inc=1, device_id={"exp": expert_at(e), "seq": seq_at(s)}, device_id_type=MESH
@@ -76,21 +80,50 @@
     ]
     for load in loads:
         load.start()
-    pl.semaphore_wait(barrier, len(partners))
-
-    up_copies = []
-    for c, (start, size) in enumerate(chunks):
-        pair = []
-        for b in (1, 2):
-            place = (pl.ds(b * cap, cap), pl.ds(start, size))
-            copy = pltpu.make_async_remote_copy(
-                src_ref=up_ref.at[place], dst_ref=ups.at[place],
-                send_sem=up_send.at[c, b - 1], recv_sem=up_recv.at[c, b - 1],
-                device_id={"exp": expert_at(-b * step)}, device_id_type=MESH,
-            )
-            copy.start()
-            pair.append(copy)
-        up_copies.append(pair)
+    pl.semaphore_wait(barrier, len(partners) + 1)
+
+    half = cap // 2
+    near_to = (step == 1) & (lax.rem(exp, 2) == 1)
+    near_from = (step == 1) & (lax.rem(exp, 2) == 0)
+
+    def share(c, b, which):
+        return (
+            pl.ds(pl.multiple_of(b * cap + which * half, half), half),
+            pl.ds(pl.multiple_of(c * size, 128), size),
+        )
+
+    def direct(c, b):
+        place = share(c, b, side)
+        return pltpu.make_async_remote_copy(
+            src_ref=up_ref.at[place], dst_ref=ups.at[place],
+            send_sem=up_send.at[c, b - 1], recv_sem=up_recv.at[c, b - 1],
+            device_id={"exp": expert_at(-b * step)}, device_id_type=MESH,
+        )
+
+    def near(c):
+        place = share(c, 1, 1 - side)
+        return pltpu.make_async_remote_copy(
+            src_ref=up_ref.at[place], dst_ref=ups.at[place],
+            send_sem=near_send.at[c], recv_sem=far_recv.at[c, 0],
+            device_id={"exp": expert_at(-step)}, device_id_type=MESH,
+        )
+
+    def forward(c, b, which):
+        place = share(c, b, which)
+        return pltpu.make_async_remote_copy(
+            src_ref=ups.at[place], dst_ref=ups.at[place],
+            send_sem=far_send.at[c, b - 1], recv_sem=far_recv.at[c, b - 1],
+            device_id={"dp": mate}, device_id_type=MESH,
+        )
+
+    for c in range(n_chunks):
+        direct(c, 1).start()
+        direct(c, 2).start()
+    if step == 1:
+        @pl.when(near_to)
+        def _():
+            for c in range(n_chunks):
+                near(c).start()
     og_copies = []
     for k in range(1, n_seq):
         other = seq_at(k)
@@ -126,20 +159,20 @@
         sc_copies.append(copy)
     sc[pl.ds(0, cap), :] = own_sc[pl.ds(0, cap), :]
 
-    for load in loads[1:5]:
+    for load in loads[1:4]:
         load.wait()
-    for copy in og_copies:
-        copy.wait_recv()
     t_rows = min(256, seq_len)
     factor = 1.0 / math.sqrt(HEAD_DIM)
-
-    @pl.loop(0, width // 256)
+    pairs = width // 256
+    per_pair = -(-n_chunks // pairs)
+
+    @pl.loop(0, pairs)
     def _(pair):
         columns = pl.ds(pl.multiple_of(pair * 256, 256), 256)
         keys = dot_of(lat_v[...], kw_v[:, columns]).astype(jnp.bfloat16)
-        for half in range(2):
-            head = pl.ds(pl.multiple_of(pair * 256 + half * HEAD_DIM, HEAD_DIM), HEAD_DIM)
-            k_head = keys[:, half * HEAD_DIM : (half + 1) * HEAD_DIM]
+        for member in range(2):
+            head = pl.ds(pl.multiple_of(pair * 256 + member * HEAD_DIM, HEAD_DIM), HEAD_DIM)
+            k_head = keys[:, member * HEAD_DIM : (member + 1) * HEAD_DIM]
             for first in range(0, seq_len, t_rows):
                 last = first + t_rows
                 q_head = q_v[pl.ds(first, t_rows), head]
@@ -151,18 +184,29 @@
                 scores = jnp.where(u <= t, scores, -jnp.inf)
                 weights = jnp.exp(scores - scores.max(axis=0, keepdims=True))
                 probs = weights * (1.0 / weights.sum(axis=0, keepdims=True))
-                term = dot_of(probs.astype(jnp.bfloat16), g_v[pl.ds(first, t_rows), head])
-                total = term if first == 0 else term + jnp.concatenate(
-                    [total, jnp.zeros((t_rows, HEAD_DIM), jnp.float32)], 0
+                probs_v[2 * pair + member, pl.ds(0, last), pl.ds(first, t_rows)] = probs.astype(
+                    jnp.bfloat16
                 )
-            vg_ref[:, head] = total.astype(jnp.bfloat16)
+        for i in range(per_pair):
+            c = pair * per_pair + i
+
+            @pl.when(c < n_chunks)
+            def _():
+                for b in (2, 1):
+                    direct(c, b).wait_recv()
+                    if b == 1 and step == 1:
+                        @pl.when(jnp.logical_not(near_from))
+                        def _():
+                            forward(c, b, side).start()
+                    else:
+                        forward(c, b, side).start()
 
     loads[5].wait()
     loads[6].wait()
-    for c, (start, size) in enumerate(chunks):
-        for copy in up_copies[c]:
-            copy.wait_recv()
-        columns = pl.ds(start, size)
+    for c in range(n_chunks):
+        for b in (1, 2):
+            forward(c, b, 1 - side).wait_recv()
+        columns = pl.ds(c * size, size)
         product = lax.dot_general(
             ups[:, columns], w_v[:, columns], LAST, preferred_element_type=jnp.float32
         )
@@ -200,6 +244,24 @@
             def _():
                 recv[seq, pl.ds(place, count)] = part[pl.ds(first, count)]
 
+    loads[4].wait()
+    for copy in og_copies:
+        copy.wait_recv()
+
+    @pl.loop(0, width // HEAD_DIM)
+    def _(h):
+        head = pl.ds(pl.multiple_of(h * HEAD_DIM, HEAD_DIM), HEAD_DIM)
+        total = None
+        for first in range(0, seq_len, t_rows):
+            term = dot_of(
+                probs_v[h, pl.ds(0, first + t_rows), pl.ds(first, t_rows)],
+                g_v[pl.ds(first, t_rows), head],
+            )
+            total = term if first == 0 else term + jnp.concatenate(
+                [total, jnp.zeros((t_rows, HEAD_DIM), jnp.float32)], 0
+            )
+        vg_ref[:, head] = total.astype(jnp.bfloat16)
+
     for copy in sc_copies:
         copy.wait_recv()
     sc_t[...] = sc[...].astype(jnp.float32).T.astype(jnp.bfloat16)
@@ -229,8 +291,19 @@
             @pl.when(seq != owner)
             def _():
                 group_copy(n).wait_send()
-    for copy in sc_copies + og_copies + [c for pair in up_copies for c in pair]:
+    for copy in sc_copies + og_copies:
         copy.wait_send()
+    for c in range(n_chunks):
+        direct(c, 1).wait_send()
+        direct(c, 2).wait_send()
+        forward(c, 2, side).wait_send()
+        if step == 1:
+            @pl.when(near_to)
+            def _():
+                near(c).wait_send()
+                forward(c, 1, side).wait_send()
+        else:
+            forward(c, 1, side).wait_send()
 
 
 def on_device(
@@ -246,14 +319,14 @@
     granule, groups = grad_groups(rows // BLOCKS, rows_per)
     size = 512 if model % 512 == 0 else model
     tile = 512 if model % 512 == 0 else 128
-    chunks = [(start, size) for start in range(0, model, size)]
+    n_chunks = model // size
     bf16, f32 = jnp.bfloat16, jnp.float32
     anywhere = pl.BlockSpec(memory_space=pltpu.HBM)
     vmem = pl.BlockSpec(memory_space=pltpu.VMEM)
     smem = pl.BlockSpec(memory_space=pltpu.SMEM)
     dma = pltpu.SemaphoreType.DMA
     value_grad, hidden_grad, weight_grad = pl.pallas_call(
-        functools.partial(kernel, n_exp, n_seq, chunks, tile, granule, groups),
+        functools.partial(kernel, n_exp, n_seq, size, tile, granule, groups),
         out_shape=(
             pltpu.VMEM((seq_len, width), bf16),
             pltpu.VMEM((rows_per, hidden), f32),
@@ -276,11 +349,15 @@
             pltpu.VMEM((rows, hidden), f32),
             pltpu.VMEM((rows // granule, granule, hidden), bf16),
             pltpu.VMEM((n_seq, rows_per // granule, granule, hidden), bf16),
+            pltpu.VMEM((width // HEAD_DIM, seq_len, seq_len), bf16),
             dma((7,)),
             dma((n_seq - 1,)),
             dma((n_seq - 1,)),
-            dma((len(chunks), 2)),
-            dma((len(chunks), 2)),
+            dma((n_chunks, 2)),
+            dma((n_chunks, 2)),
+            dma((n_chunks,)),
+            dma((n_chunks, 2)),
+            dma((n_chunks, 2)),
             dma((2,)),
             dma((2,)),
             dma((len(groups),)),

time: 30.2 us -> 27.4 us (0.907)
  Pallas kernels: 26.1 us -> 23.3 us
    pallas_call x1, Pallas kernels: 26.1 us -> 23.3 us  [on_device(): pl.pallas_call(functools.partial(kernel, n_exp, n_seq, size, tile, granul...]
where the time goes in v2:
time: 27.4 us; the launch traced here: 27.3 us
  Pallas kernels  23.3 us (85%)
  local copies, waits for them, and re-layouts  3.31 us (12%)
  between operations  0.64 us (2%)
    pallas_call x1, Pallas kernels, on_device(): pl.pallas_call(functools.partial(kernel, n_exp, n_seq, size, tile, granul...  23.3 us
    unnamed x3, local copies, waits for them, and re-layouts  3.31 us

profile of v2, /device:TPU:0, one launch (start us, length us, event | category | flops | bytes accessed | tf_op | source)
XLA Modules:
  0.0 27.3 jit_solution(4522870918439481687)
XLA Ops:
  0.6 23.3 %shard_map.112 = (bf16[256,1024]{1,0:T(8,128)(2,1)S(1)}, f32[96,512]{1,0:T(8,128)S(1)}, bf16[512,3584]{1,0:T(8,128)(2,1)S(1)}) custom-call(bf16[256,1024]{1,0:T(8,128)(2,1)} %bitcast.12, bf16[256,512]{1,0:T(8,128)(2,1)} %bitcast.14, bf16[512,1024]{1,0:T(8,128)(2,1)} %bitcast.11, bf16[128,2048]{1,0:T(8,128)(2,1)} %bitcast.13, bf16[512,3584]{1,0:T(8,128)(2,1)} %bitcast.10, ...), custom_call_target="tpu_custom_call" | custom-call | tf_op jit(solution)/shard_map/pallas_call | solution.py:328
  24.0 0.8 %copy.15 = bf16[1,256,1,1024]{3,1,2,0:T(8,128)(2,1)} copy(bf16[1,256,1,1024]{3,1,2,0:T(8,128)(2,1)S(1)} %bitcast.9) | data formatting | bytes 1048576
  24.8 0.7 %copy.16 = f32[96,512]{1,0:T(8,128)} copy(f32[96,512]{1,0:T(8,128)S(1)} %get-tuple-element.10) | data formatting | bytes 393216
  25.4 1.8 %copy.17 = bf16[1,512,3584]{2,1,0:T(8,128)(2,1)} copy(bf16[1,512,3584]{2,1,0:T(8,128)(2,1)S(1)} %bitcast.8) | data formatting | bytes 7340032

commit v3 on v2

--- a/solution.py
+++ b/solution.py
@@ -201,49 +201,6 @@
                     else:
                         forward(c, b, side).start()
 
-    loads[5].wait()
-    loads[6].wait()
-    for c in range(n_chunks):
-        for b in (1, 2):
-            forward(c, b, 1 - side).wait_recv()
-        columns = pl.ds(c * size, size)
-        product = lax.dot_general(
-            ups[:, columns], w_v[:, columns], LAST, preferred_element_type=jnp.float32
-        )
-        acc[...] = product if c == 0 else acc[...] + product
-    part[...] = acc[...].reshape(part.shape).astype(jnp.bfloat16)
-
-    def group_copy(n):
-        block, first, count, owner, place = groups[n]
-        return pltpu.make_async_remote_copy(
-            src_ref=part.at[pl.ds(first, count)],
-            dst_ref=recv.at[seq, pl.ds(place, count)],
-            send_sem=part_send.at[n], recv_sem=part_recv.at[seq, n],
-            device_id={"exp": expert_at(block * step), "seq": owner}, device_id_type=MESH,
-        )
-
-    def arrival(n, source):
-        block, first, count, owner, place = groups[n]
-        return pltpu.make_async_remote_copy(
-            src_ref=part.at[pl.ds(first, count)],
-            dst_ref=recv.at[source, pl.ds(place, count)],
-            send_sem=part_send.at[n], recv_sem=part_recv.at[source, n],
-            device_id={"exp": expert_at(block * step), "seq": owner}, device_id_type=MESH,
-        )
-
-    for n in reversed(range(len(groups))):
-        block, first, count, owner, place = groups[n]
-        if block:
-            group_copy(n).start()
-        else:
-            @pl.when(seq != owner)
-            def _():
-                group_copy(n).start()
-
-            @pl.when(seq == owner)
-            def _():
-                recv[seq, pl.ds(place, count)] = part[pl.ds(first, count)]
-
     loads[4].wait()
     for copy in og_copies:
         copy.wait_recv()
@@ -262,14 +219,64 @@
             )
         vg_ref[:, head] = total.astype(jnp.bfloat16)
 
-    for copy in sc_copies:
-        copy.wait_recv()
-    sc_t[...] = sc[...].astype(jnp.float32).T.astype(jnp.bfloat16)
-
-    @pl.loop(0, w_ref.shape[1] // tile)
-    def _(n):
-        columns = pl.ds(pl.multiple_of(n * tile, tile), tile)
-        wg_ref[:, columns] = dot_of(sc_t[...], ups[:, columns]).astype(jnp.bfloat16)
+    lag = 3
+
+    def weigh(c):
+        if c == 0:
+            for copy in sc_copies:
+                copy.wait_recv()
+            sc_t[...] = sc[...].astype(jnp.float32).T.astype(jnp.bfloat16)
+        for start in range(c * size, (c + 1) * size, tile):
+            columns = pl.ds(start, tile)
+            wg_ref[:, columns] = dot_of(sc_t[...], ups[:, columns]).astype(jnp.bfloat16)
+
+    loads[5].wait()
+    loads[6].wait()
+    for c in range(n_chunks):
+        for b in (1, 2):
+            forward(c, b, 1 - side).wait_recv()
+        columns = pl.ds(c * size, size)
+        product = lax.dot_general(
+            ups[:, columns], w_v[:, columns], LAST, preferred_element_type=jnp.float32
+        )
+        acc[...] = product if c == 0 else acc[...] + product
+        if c >= lag:
+            weigh(c - lag)
+    part[...] = acc[...].reshape(part.shape).astype(jnp.bfloat16)
+
+    def group_copy(n):
+        block, first, count, owner, place = groups[n]
+        return pltpu.make_async_remote_copy(
+            src_ref=part.at[pl.ds(first, count)],
+            dst_ref=recv.at[seq, pl.ds(place, count)],
+            send_sem=part_send.at[n], recv_sem=part_recv.at[seq, n],
+            device_id={"exp": expert_at(block * step), "seq": owner}, device_id_type=MESH,
+        )
+
+    def arrival(n, source):
+        block, first, count, owner, place = groups[n]
+        return pltpu.make_async_remote_copy(
+            src_ref=part.at[pl.ds(first, count)],
+            dst_ref=recv.at[source, pl.ds(place, count)],
+            send_sem=part_send.at[n], recv_sem=part_recv.at[source, n],
+            device_id={"exp": expert_at(block * step), "seq": owner}, device_id_type=MESH,
+        )
+
+    for n in reversed(range(len(groups))):
+        block, first, count, owner, place = groups[n]
+        if block:
+            group_copy(n).start()
+        else:
+            @pl.when(seq != owner)
+            def _():
+                group_copy(n).start()
+
+            @pl.when(seq == owner)
+            def _():
+                recv[seq, pl.ds(place, count)] = part[pl.ds(first, count)]
+
+    for c in range(max(0, n_chunks - lag), n_chunks):
+        weigh(c)
 
     for n, (block, first, count, owner, place) in enumerate(groups):
         for source in range(n_seq):

time: 27.4 us -> 27.6 us (level)
  no operation moved by 1% of the time
where the time goes in v3:
time: 27.6 us; the launch traced here: 27.4 us
  Pallas kernels  23.5 us (85%)
  local copies, waits for them, and re-layouts  3.31 us (12%)
  between operations  0.64 us (2%)
    pallas_call x1, Pallas kernels, on_device(): pl.pallas_call(functools.partial(kernel, n_exp, n_seq, size, tile, granul...  23.5 us
    unnamed x3, local copies, waits for them, and re-layouts  3.31 us

profile of v3, /device:TPU:0, one launch (start us, length us, event | category | flops | bytes accessed | tf_op | source)
XLA Modules:
  0.0 27.4 jit_solution(16251994304887651439)
XLA Ops:
  0.6 23.5 %shard_map.112 = (bf16[256,1024]{1,0:T(8,128)(2,1)S(1)}, f32[96,512]{1,0:T(8,128)S(1)}, bf16[512,3584]{1,0:T(8,128)(2,1)S(1)}) custom-call(bf16[256,1024]{1,0:T(8,128)(2,1)} %bitcast.12, bf16[256,512]{1,0:T(8,128)(2,1)} %bitcast.14, bf16[512,1024]{1,0:T(8,128)(2,1)} %bitcast.11, bf16[128,2048]{1,0:T(8,128)(2,1)} %bitcast.13, bf16[512,3584]{1,0:T(8,128)(2,1)} %bitcast.10, ...), custom_call_target="tpu_custom_call" | custom-call | tf_op jit(solution)/shard_map/pallas_call | solution.py:335
  24.1 0.8 %copy.15 = bf16[1,256,1,1024]{3,1,2,0:T(8,128)(2,1)} copy(bf16[1,256,1,1024]{3,1,2,0:T(8,128)(2,1)S(1)} %bitcast.9) | data formatting | bytes 1048576
  24.9 0.7 %copy.16 = f32[96,512]{1,0:T(8,128)} copy(f32[96,512]{1,0:T(8,128)S(1)} %get-tuple-element.10) | data formatting | bytes 393216
  25.6 1.8 %copy.17 = bf16[1,512,3584]{2,1,0:T(8,128)(2,1)} copy(bf16[1,512,3584]{2,1,0:T(8,128)(2,1)S(1)} %bitcast.8) | data formatting | bytes 7340032
